TPU v7x, 32 devices: a whole 2x2x4 slice. The times are simulated.
32 devices in a mesh: row: 16 (over z, x, core), col: 2 (over y).
Axes of the slice: x: 2, y: 2, z: 4, core: 2. Of those that a mesh axis runs over, the one named last changes fastest.
Arguments:
- gbar: float32 [8192, 8192], P('row', 'col'), may hold values from -9 to 9
- panels: float32 [8192, 1024], P('row'), may hold values from -0.0625 to 0.0625
- panel_cot: float32 [8192, 1024], P('row'), may hold values from -6 to 6
- inverses: float32 [2, 512, 512], replicated, may hold values from -1 to 2, as said below
Outputs:
- adjoint: float32 [8192, 1024], P('row')
- diag_adjoint: float32 [2, 512, 512], P(None, 'row')
Inputs may be any that keep to these rules, and one draw needn't show every extreme that they name: Each inverses[i] is lower triangular with diagonal entries between 1 and 2.
All inputs are finite; a program needn't handle non-finite values.
Results may differ from a plain program's by a relative error of at most 0.000071.
Values sent between devices are 32-bit elements; how exact they have to be, the bound alone decides.
A program may use at most 128 MiB of HBM per device.

v0:
```python
import jax
import jax.numpy as jnp
from jax import lax
from jax.sharding import PartitionSpec as P


def spread(value, axis, source):
    kept = jnp.where(lax.axis_index(axis) == source, value, 0).astype(value.dtype)
    return lax.psum(kept, axis)


def per_device(gbar, panels, panel_cot, inverses):
    width = inverses.shape[-1]
    exact_mode = lax.Precision.HIGHEST
    row_id = lax.axis_index("row")
    col_count = lax.axis_size("col")
    partial_value = lax.dot_general(
        gbar,
        panels,
        (((0,), (0,)), ((), ())),
        precision=exact_mode,
        preferred_element_type=jnp.float32,
    )
    summed = lax.psum(partial_value, "row")
    own_tile = lax.dynamic_slice_in_dim(summed, row_id // col_count * width, width, 0)
    coupled = spread(own_tile, "col", row_id % col_count)
    combined = panel_cot - 2.0 * coupled
    first_adj = jnp.dot(
        combined[:, :width], inverses[0], precision=exact_mode, preferred_element_type=jnp.float32
    )
    second_adj = jnp.dot(
        combined[:, width:], inverses[1], precision=exact_mode, preferred_element_type=jnp.float32
    )
    adjoint = jnp.concatenate([first_adj, second_adj], axis=1)
    contract = (((0,), (0,)), ((), ()))
    first_diag = -lax.dot_general(
        first_adj,
        panels[:, :width],
        contract,
        precision=exact_mode,
        preferred_element_type=jnp.float32,
    )
    second_diag = -lax.dot_general(
        second_adj,
        panels[:, width:],
        contract,
        precision=exact_mode,
        preferred_element_type=jnp.float32,
    )
    diag_terms = jnp.stack([first_diag, second_diag])
    diag_adjoint = lax.psum_scatter(diag_terms, "row", scatter_dimension=1, tiled=True)
    return (adjoint, diag_adjoint)


def solution(mesh):
    in_specs = (P("row", "col"), P("row", None), P("row", None), P())
    out_specs = (P("row", None), P(None, "row", None))
    return jax.shard_map(
        per_device, mesh=mesh, in_specs=in_specs, out_specs=out_specs, check_vma=False
    )
```

profile of v0, /device:TPU:0, one launch (start us, length us, event | category | flops | bytes accessed | tf_op | source)
XLA Modules:
  0.0 485.4 jit_solution(16080054003184823967)
XLA Ops:
  7.2 0.0 all-reduce.3.cloned.1.call-start
  7.2 31.4 %fusion.12 = f32[4096,1024]{1,0:T(8,128)} fusion(f32[512,4096]{1,0:T(8,128)} %param.4, f32[512,1024]{1,0:T(8,128)} %param.5), kind=kOutput, calls=%fused_computation.18 | convolution fusion | flops 25769803776 | bytes 27262976 | tf_op jit(solution)/shard_map/dot_general | solution.py:17
  38.6 0.0 all-reduce.3.cloned.1.call-update
  38.6 0.0 all-reduce.5.cloned.1.call-start
  38.7 301.0 %all-reduce.3.cloned.1.call-done = f32[4096,1024]{1,0:T(8,128)} async-done(((f32[4096,1024]{1,0:T(8,128)}), f32[4096,1024]{1,0:T(8,128)}) %all-reduce.3.cloned.1.call-update) | async-done | bytes 16777232 | tf_op jit(solution)/shard_map/psum | solution.py:24
  339.8 3.2 dynamic-slice_select_fusion
  343.0 0.0 copy-start.1
  343.0 0.0 all-reduce.5.cloned.1.call-update
  343.0 0.2 reduce-scatter.2.cloned.1.call-start
  343.2 62.6 %all-reduce.5.cloned.1.call-done = f32[512,1024]{1,0:T(8,128)} async-done(((f32[512,1024]{1,0:T(8,128)}), f32[512,1024]{1,0:T(8,128)}) %all-reduce.5.cloned.1.call-update) | async-done | bytes 2097168 | tf_op jit(solution)/shard_map/psum | solution.py:9
  405.8 0.0 copy-done.1
  405.8 0.0 copy-start.2
  405.8 2.2 multiply_subtract_fusion
  408.0 0.1 copy-done.2
  408.0 1.9 fusion.2
  409.9 0.0 copy-start
  410.0 1.9 fusion.4
  411.9 0.0 copy-done
  411.9 1.9 fusion
  413.7 1.9 fusion.1
  415.6 1.5 pad_maximum_fusion.1
  417.1 0.0 reduce-scatter.2.cloned.1.call-update
  417.1 1.5 pad_maximum_fusion
  418.6 2.9 copy.6
  421.5 57.3 %reduce-scatter.2.cloned.1.call-done = f32[2,32,512]{2,1,0:T(8,128)} async-done(((f32[2,512,512]{2,1,0:T(8,128)}), f32[2,32,512]{2,1,0:T(8,128)}) %reduce-scatter.2.cloned.1.call-update) | async-done | bytes 131088 | tf_op jit(solution)/shard_map/reduce_scatter | solution.py:51
Async XLA Ops:
  7.2 332.6 %all-reduce.3.cloned.1.call-start = ((), (), s32[]{:S(2)}) async-start(), calls=%async_computation.1 | async-start | bytes 33554432 | tf_op jit(solution)/shard_map/psum | solution.py:24
  38.6 367.2 %all-reduce.5.cloned.1.call-start = ((), (), s32[]{:S(2)}) async-start(), calls=%async_computation.2 | async-start | bytes 4194304 | tf_op jit(solution)/shard_map/psum | solution.py:9
  343.0 62.9 %copy-start.1 = (f32[512,1024]{1,0:T(8,128)S(1)}, f32[512,1024]{1,0:T(8,128)}, u32[]{:S(2)}) copy-start(f32[512,1024]{1,0:T(8,128)} %param.6) | copy-start | bytes 6291460
  343.0 135.9 %reduce-scatter.2.cloned.1.call-start = ((), (), s32[]{:S(2)}) async-start(), calls=%async_computation.3 | async-start | bytes 2228224 | tf_op jit(solution)/shard_map/reduce_scatter | solution.py:51
  405.8 2.2 copy-start.2
  409.9 1.9 copy-start
Sparse Core Ops, SparseCore 0:
  38.8 300.9 all-reduce.2
  343.1 62.6 all-reduce.4
  417.3 61.5 reduce-scatter.1
where the time goes:
time: 486 us; the launch traced here: 485 us
  waiting for transfers between devices  421 us (87%)
  matrix products  38.9 us (8%)
  between operations  13.8 us (3%)
  other arithmetic  8.34 us (2%)
    psum x1, waiting for transfers between devices, per_device(): summed = lax.psum(partial_value, 'row')  301 us
    psum x1, waiting for transfers between devices, spread(): return lax.psum(kept, axis)  62.6 us
    reduce_scatter x1, waiting for transfers between devices, per_device(): lax.psum_scatter(diag_terms, 'row', scatter_dimension=1, tiled=True)  57.3 us
    dot_general x1, matrix products, per_device(): lax.dot_general(gbar, panels, (((0,), (0,)), ((), ())), precision=exact_m...  31.4 us
  transfers between devices with their start and end apart: 3, of which 3 were waited for; matrix products, arithmetic and copies ran while one was open for 1% of the time, Pallas kernels for 0%

commit v1 on v0

--- a/solution.py
+++ b/solution.py
@@ -21,7 +21,10 @@
         precision=exact_mode,
         preferred_element_type=jnp.float32,
     )
-    summed = lax.psum(partial_value, "row")
+    size, summed = (lax.axis_size("row"), partial_value)
+    for far in [1 << k for k in range(size.bit_length() - 1)]:
+        swap = [(i, i ^ far) for i in range(size)]
+        summed = summed + lax.ppermute(summed, "row", swap)
     own_tile = lax.dynamic_slice_in_dim(summed, row_id // col_count * width, width, 0)
     coupled = spread(own_tile, "col", row_id % col_count)
     combined = panel_cot - 2.0 * coupled

time: 486 us -> 1700 us (3.50)
  waiting for transfers between devices: 421 us -> 1590 us
  other arithmetic: 8.34 us -> 46 us
    ppermute x0 -> x4, waiting for transfers between devices: none -> 1460 us  [per_device(): summed = summed + lax.ppermute(summed, 'row', swap)]
    psum x1 -> x0, waiting for transfers between devices: 301 us -> none  [per_device(): summed = lax.psum(partial_value, 'row')]
    add x0 -> x3, other arithmetic: none -> 36.6 us  [per_device(): summed = summed + lax.ppermute(summed, 'row', swap)]
  transfers between devices with their start and end apart: 3 -> 6, of which waited for: 3 -> 6; matrix products, arithmetic and copies ran while one was open for 1% -> 0% of each run, Pallas kernels for 0% -> 0%
where the time goes in v1:
time: 1700 us
  waiting for transfers between devices  1590 us (94%)
  other arithmetic  46 us (3%)
  matrix products  38.7 us (2%)
    ppermute x4, waiting for transfers between devices, per_device(): summed = summed + lax.ppermute(summed, 'row', swap)  1460 us
    psum x1, waiting for transfers between devices, spread(): return lax.psum(kept, axis)  63.6 us
    reduce_scatter x1, waiting for transfers between devices, per_device(): lax.psum_scatter(diag_terms, 'row', scatter_dimension=1, tiled=True)  57.3 us
    add x3, other arithmetic, per_device(): summed = summed + lax.ppermute(summed, 'row', swap)  36.6 us
  transfers between devices with their start and end apart: 6, of which 6 were waited for; matrix products, arithmetic and copies ran while one was open for 0% of the time, Pallas kernels for 0%

profile of v1, /device:TPU:0, one launch (start us, length us, event | category | flops | bytes accessed | tf_op | source)
XLA Modules:
  0.0 1695.5 jit_solution(12458530291625175999)
XLA Ops:
  7.2 0.0 all-reduce.2.cloned.1.call-start
  7.2 31.1 %fusion.13 = f32[4096,1024]{1,0:T(8,128)S(1)} fusion(f32[512,4096]{1,0:T(8,128)} %param.4, f32[512,1024]{1,0:T(8,128)} %param.5), kind=kOutput, calls=%fused_computation.19 | convolution fusion | flops 25769803776 | bytes 27262976 | tf_op jit(solution)/shard_map/dot_general | solution.py:17
  38.4 0.5 collective-permute-start
  38.9 24.9 %collective-permute-done = f32[4096,1024]{1,0:T(8,128)} collective-permute-done((f32[4096,1024]{1,0:T(8,128)S(1)}, f32[4096,1024]{1,0:T(8,128)}, u32[]{:S(2)}, u32[]{:S(2)}) %collective-permute-start) | collective-permute-done | bytes 16777248 | tf_op jit(solution)/shard_map/ppermute | solution.py:27
  63.8 12.4 add.25
  76.2 2.9 collective-permute-start.1
  79.1 360.8 %collective-permute-done.1 = f32[4096,1024]{1,0:T(8,128)} collective-permute-done((f32[4096,1024]{1,0:T(8,128)}, f32[4096,1024]{1,0:T(8,128)}, u32[]{:S(2)}, u32[]{:S(2)}) %collective-permute-start.1) | collective-permute-done | bytes 16777248 | tf_op jit(solution)/shard_map/ppermute | solution.py:27
  439.9 11.8 add.26
  451.7 1.9 collective-permute-start.2
  453.6 360.0 %collective-permute-done.2 = f32[4096,1024]{1,0:T(8,128)} collective-permute-done((f32[4096,1024]{1,0:T(8,128)S(1)}, f32[4096,1024]{1,0:T(8,128)}, u32[]{:S(2)}, u32[]{:S(2)}) %collective-permute-start.2) | collective-permute-done | bytes 16777248 | tf_op jit(solution)/shard_map/ppermute | solution.py:27
  813.6 12.4 add.27
  826.0 2.5 collective-permute-start.3
  828.6 719.1 %collective-permute-done.3 = f32[4096,1024]{1,0:T(8,128)} collective-permute-done((f32[4096,1024]{1,0:T(8,128)}, f32[4096,1024]{1,0:T(8,128)}, u32[]{:S(2)}, u32[]{:S(2)}) %collective-permute-start.3) | collective-permute-done | bytes 16777248 | tf_op jit(solution)/shard_map/ppermute | solution.py:27
  1547.6 4.2 fusion
  1551.8 0.0 copy-start.1
  1551.8 0.0 all-reduce.2.cloned.1.call-update
  1551.8 0.2 reduce-scatter.2.cloned.1.call-start
  1552.1 63.6 %all-reduce.2.cloned.1.call-done = f32[512,1024]{1,0:T(8,128)} async-done(((f32[512,1024]{1,0:T(8,128)}), f32[512,1024]{1,0:T(8,128)}) %all-reduce.2.cloned.1.call-update) | async-done | bytes 2097168 | tf_op jit(solution)/shard_map/psum | solution.py:9
  1615.6 0.0 copy-done.1
  1615.6 0.0 copy-start.2
  1615.6 2.2 multiply_subtract_fusion
  1617.8 0.1 copy-done.2
  1617.9 1.9 fusion.3
  1619.8 0.0 copy-start
  1619.8 1.9 fusion.5
  1621.7 0.0 copy-done
  1621.7 1.9 fusion.2
  1623.6 1.9 fusion.1
  1625.4 1.5 pad_maximum_fusion.1
  1627.0 0.0 reduce-scatter.2.cloned.1.call-update
  1627.0 1.5 pad_maximum_fusion
  1628.5 2.9 copy.6
  1631.3 57.3 %reduce-scatter.2.cloned.1.call-done = f32[2,32,512]{2,1,0:T(8,128)} async-done(((f32[2,512,512]{2,1,0:T(8,128)}), f32[2,32,512]{2,1,0:T(8,128)}) %reduce-scatter.2.cloned.1.call-update) | async-done | bytes 131088 | tf_op jit(solution)/shard_map/reduce_scatter | solution.py:54
Async XLA Ops:
  7.2 1608.5 %all-reduce.2.cloned.1.call-start = ((), (), s32[]{:S(2)}) async-start(), calls=%async_computation.1 | async-start | bytes 4194304 | tf_op jit(solution)/shard_map/psum | solution.py:9
  38.4 25.4 %collective-permute-start = (f32[4096,1024]{1,0:T(8,128)S(1)}, f32[4096,1024]{1,0:T(8,128)}, u32[]{:S(2)}, u32[]{:S(2)}) collective-permute-start(f32[4096,1024]{1,0:T(8,128)S(1)} %fusion.13), channel_id=1, source_target_pairs={{0,2},{2,0},{4,6},{6,4},{8,10},{10,8},{12,14},{14,12},{16,18},{18,... | collective-permute-start | bytes 50331656 | tf_op jit(solution)/shard_map/ppermute | solution.py:27
  76.2 363.7 %collective-permute-start.1 = (f32[4096,1024]{1,0:T(8,128)}, f32[4096,1024]{1,0:T(8,128)}, u32[]{:S(2)}, u32[]{:S(2)}) collective-permute-start(f32[4096,1024]{1,0:T(8,128)} %add.25), channel_id=1, source_target_pairs={{0,4},{2,6},{4,0},{6,2},{8,12},{10,14},{12,8},{14,10},{16,20},{18,... | collective-permute-start | bytes 50331656 | tf_op jit(solution)/shard_map/ppermute | solution.py:27
  451.7 361.9 %collective-permute-start.2 = (f32[4096,1024]{1,0:T(8,128)S(1)}, f32[4096,1024]{1,0:T(8,128)}, u32[]{:S(2)}, u32[]{:S(2)}) collective-permute-start(f32[4096,1024]{1,0:T(8,128)S(1)} %add.26), channel_id=1, source_target_pairs={{0,8},{2,10},{4,12},{6,14},{8,0},{10,2},{12,4},{14,6},{16,24},{18,... | collective-permute-start | bytes 50331656 | tf_op jit(solution)/shard_map/ppermute | solution.py:27
  826.0 721.6 %collective-permute-start.3 = (f32[4096,1024]{1,0:T(8,128)}, f32[4096,1024]{1,0:T(8,128)}, u32[]{:S(2)}, u32[]{:S(2)}) collective-permute-start(f32[4096,1024]{1,0:T(8,128)} %add.27), channel_id=1, source_target_pairs={{0,16},{2,18},{4,20},{6,22},{8,24},{10,26},{12,28},{14,30},{16,0},... | collective-permute-start | bytes 50331656 | tf_op jit(solution)/shard_map/ppermute | solution.py:27
  1551.8 63.8 %copy-start.1 = (f32[512,1024]{1,0:T(8,128)S(1)}, f32[512,1024]{1,0:T(8,128)}, u32[]{:S(2)}) copy-start(f32[512,1024]{1,0:T(8,128)} %param.6) | copy-start | bytes 6291460
  1551.8 136.8 %reduce-scatter.2.cloned.1.call-start = ((), (), s32[]{:S(2)}) async-start(), calls=%async_computation.2 | async-start | bytes 2228224 | tf_op jit(solution)/shard_map/reduce_scatter | solution.py:54
  1615.6 2.2 copy-start.2
  1619.8 1.9 copy-start
Sparse Core Ops, SparseCore 0:
  1552.0 63.6 all-reduce.1
  1627.1 61.5 reduce-scatter.1
